TPU v7x, 128 devices: a whole 4x4x4 slice. The times are simulated.
128 devices in a mesh: dp: 64 (over z, y, x), rep: 2 (over core).
Axes of the slice: x: 4, y: 4, z: 4, core: 2. Of those that a mesh axis runs over, the one named last changes fastest.
Arguments:
- rows_in: bfloat16 [262144, 512], P(('dp', 'rep')), may hold values from -6 to 6
- row_codes: int32 [262144], P(('dp', 'rep')), may hold values from 0 to 8191, as said below
- hot_split: int32 [256, 2], replicated, may hold values from 0 to 8191, as said below
- codebook: float32 [8192, 512], P('dp'), may hold values from -6 to 6
Outputs:
- new_codebook: float32 [8192, 512], P(('dp', 'rep'))
- next_residual: bfloat16 [262144, 512], P(('dp', 'rep'))
Inputs may be any that keep to these rules, and one draw needn't show every extreme that they name: `row_codes`: among the rows of one device, at most 48 have codes (after the split) in any one owner block codes // 128; in every draw some owner block receives exactly 48 rows from every device. `hot_split`: the hot ids are distinct; each partner differs from its hot id and lies in the same owner block (id // 128).
All inputs are finite; a program needn't handle non-finite values.
Results may differ from a plain program's by a relative error of at most 0.0055.
Values may be sent and summed in bfloat16 or wider, within the bound.
A program may use at most 64 MiB of HBM per device.

v0:
```python
import jax
import jax.numpy as jnp
from jax import lax
from jax.sharding import PartitionSpec as P

prior_weight = 8.0


def split_codes(row_codes, hot_split):
    row_number = jnp.arange(row_codes.shape[0], dtype=jnp.int32)
    is_odd = row_number % 2 == 1
    matched = row_codes[:, None] == hot_split[None, :, 0]
    is_hot = jnp.any(matched, axis=1)
    partner = jnp.sum(jnp.where(matched, hot_split[None, :, 1], 0), axis=1)
    return jnp.where(is_odd & is_hot, partner, row_codes)


def on_device(rows_in, row_codes, hot_split, codebook):
    feature_count = rows_in.shape[1]
    owner_count = lax.axis_size("dp")
    block_rows = codebook.shape[0]
    all_codes = block_rows * owner_count
    half_rows = block_rows // lax.axis_size("rep")
    codes = split_codes(row_codes, hot_split)
    my_half = lax.axis_index("rep") * half_rows
    old_half = lax.dynamic_slice_in_dim(codebook, my_half, half_rows, 0)
    residual = None
    block_size = min(512, all_codes)

    def block_sums(index_block):
        code_ids = index_block * block_size + jnp.arange(block_size, dtype=jnp.int32)
        onehot = (code_ids[:, None] == codes[None, :]).astype(jnp.bfloat16)
        partial_value = jnp.dot(onehot, rows_in, preferred_element_type=jnp.float32)
        tally = jnp.sum(onehot, axis=1, dtype=jnp.float32)
        return (partial_value, tally)

    partials, tallies = lax.map(block_sums, jnp.arange(all_codes // block_size, dtype=jnp.int32))
    partials = partials.reshape(all_codes, feature_count)
    tallies = tallies.reshape(all_codes)
    half_sums, half_counts = (
        lax.psum_scatter(partials, ("dp", "rep"), scatter_dimension=0, tiled=True),
        lax.psum_scatter(tallies, ("dp", "rep"), scatter_dimension=0, tiled=True),
    )
    new_half = (half_sums + prior_weight * old_half) / (half_counts[:, None] + prior_weight)
    half_table = new_half.astype(jnp.bfloat16)
    full_table = lax.all_gather(half_table, ("dp", "rep"), axis=0, tiled=True)
    picked = full_table[codes].astype(jnp.float32)
    residual = (rows_in.astype(jnp.float32) - picked).astype(jnp.bfloat16)
    return (new_half, residual)


def solution(mesh):
    return jax.shard_map(
        on_device,
        mesh=mesh,
        in_specs=(P(("dp", "rep"), None), P(("dp", "rep")), P(), P("dp", None)),
        out_specs=(P(("dp", "rep"), None), P(("dp", "rep"), None)),
        check_vma=False,
    )
```

profile of v0, /device:TPU:1, one launch (start us, length us, event | category | flops | bytes accessed | tf_op | source)
XLA Modules:
  0.0 864.4 jit_solution(15031335864532877525)
XLA Ops:
  7.2 0.8 fusion.20
  8.0 1.3 compare_reduce_fusion
  9.3 1.4 fusion.10
  10.8 0.7 fusion.12
  11.5 92.2 %while.12 = (s32[]{:T(128)}, f32[16,512,512]{2,1,0:T(8,128)}, f32[16,512]{1,0:T(8,128)S(1)}, s32[16]{0:T(128)S(1)}, s32[2048]{0:T(1024)S(1)}, /*index=5*/bf16[20...) while((s32[]{:T(128)}, f32[16,512,512]{2,1,0:T(8,128)}, f32[16,512]{1,0:T(8,128)S(1)}, s32[16]{0:T(128)S(1)}, ...), condition=%wide.region_4.5_spmd, body=%wide.region_2.4_spmd.sunk | while | flops 1078984704 | bytes 3175037 | solution.py:37
  11.5 0.6 dynamic_slice.11
  12.7 3.9 fusion.27
  16.6 0.5 convert_reduce_fusion.2
  17.2 0.1 dynamic_update_slice.12
  17.3 0.6 dynamic_slice.11
  18.5 3.9 fusion.27
  22.4 0.5 convert_reduce_fusion.2
  23.0 0.1 dynamic_update_slice.12
  23.1 0.6 dynamic_slice.11
  24.3 3.9 fusion.27
  28.2 0.5 convert_reduce_fusion.2
  28.7 0.1 dynamic_update_slice.12
  28.8 0.6 dynamic_slice.11
  30.1 3.9 fusion.27
  33.9 0.5 convert_reduce_fusion.2
  34.5 0.1 dynamic_update_slice.12
  34.6 0.6 dynamic_slice.11
  35.8 3.9 fusion.27
  39.7 0.5 convert_reduce_fusion.2
  40.3 0.6 dynamic_slice.11
  41.6 3.9 fusion.27
  45.5 0.5 convert_reduce_fusion.2
  46.1 0.6 dynamic_slice.11
  47.3 3.9 fusion.27
  51.2 0.5 convert_reduce_fusion.2
  51.9 0.6 dynamic_slice.11
  53.1 3.9 fusion.27
  57.0 0.5 convert_reduce_fusion.2
  57.6 0.6 dynamic_slice.11
  58.9 4.0 fusion.27
  62.8 0.5 convert_reduce_fusion.2
  63.5 0.6 dynamic_slice.11
  64.7 3.9 fusion.27
  68.6 0.5 convert_reduce_fusion.2
  69.2 0.6 dynamic_slice.11
  70.4 3.9 fusion.27
  74.3 0.5 convert_reduce_fusion.2
  74.9 0.6 dynamic_slice.11
  76.2 3.9 fusion.27
  80.0 0.5 convert_reduce_fusion.2
  80.7 0.6 dynamic_slice.11
  81.9 3.9 fusion.27
  85.9 0.5 convert_reduce_fusion.2
  86.5 0.6 dynamic_slice.11
  87.7 3.9 fusion.27
  91.6 0.5 convert_reduce_fusion.2
  92.2 0.6 dynamic_slice.11
  93.5 3.9 fusion.27
  97.3 0.5 convert_reduce_fusion.2
  98.0 0.6 dynamic_slice.11
  99.2 3.9 fusion.27
  103.1 0.5 convert_reduce_fusion.2
  103.9 69.8 %all-reduce = f32[8192]{0:T(1024)S(1)} all-reduce(f32[8192]{0:T(1024)S(1)} %bitcast.21), channel_id=3, replica_groups=mesh['dp'=64,'rep'=2] {'dp','rep'}, use_global_device_ids=true, to_apply=%region_6.7.clone | all-reduce | flops 8192 | bytes 65536
  173.7 0.1 dynamic-slice_add_fusion
  173.8 593.5 %reduce-scatter.2.cloned.1.call-done = f32[64,512]{1,0:T(8,128)} async-done(((f32[8192,512]{1,0:T(8,128)}), f32[64,512]{1,0:T(8,128)}) %reduce-scatter.2.cloned.1.call-update) | async-done | bytes 131088 | tf_op jit(solution)/shard_map/reduce_scatter | solution.py:41
  767.2 1.7 fusion.19
  768.9 73.1 %all-gather.2.cloned.1.call-done = bf16[8192,512]{1,0:T(8,128)(2,1)} async-done(((bf16[64,512]{1,0:T(8,128)(2,1)}), bf16[8192,512]{1,0:T(8,128)(2,1)}) %all-gather.2.cloned.1.call-update) | async-done | bytes 8388624 | tf_op jit(solution)/shard_map/all_gather | solution.py:46
  842.0 12.0 %gather_fusion = bf16[2048,512]{1,0:T(8,128)(2,1)S(1)} fusion(bf16[8192,512]{1,0:T(8,128)(2,1)} %all-gather.2.cloned.1.call-done, s32[2048]{0:T(1024)S(1)} %get-tuple-element.49), kind=kCustom, calls=%fused_computation | custom fusion | bytes 4202496 | tf_op jit(solution)/shard_map/gather | solution.py:47
  854.0 3.5 subtract_convert_fusion
  (38 shorter events, 0.9 us)
Async XLA Ops:
  7.2 760.1 %reduce-scatter.2.cloned.1.call-start = ((), (), s32[]{:S(2)}) async-start(), calls=%async_computation.1 | async-start | bytes 16908288 | tf_op jit(solution)/shard_map/reduce_scatter | solution.py:41
  103.7 663.5 %copy-start = (f32[128,512]{1,0:T(8,128)S(1)}, f32[128,512]{1,0:T(8,128)}, u32[]{:S(2)}) copy-start(f32[128,512]{1,0:T(8,128)} %param.9) | copy-start | bytes 786436
  103.8 738.2 %all-gather.2.cloned.1.call-start = ((), (), s32[]{:S(2)}) async-start(), calls=%async_computation.2 | async-start | bytes 8454144 | tf_op jit(solution)/shard_map/all_gather | solution.py:46
Sparse Core Ops, SparseCore 0:
  103.9 663.2 reduce-scatter.1
  770.8 71.1 all-gather.1
where the time goes:
time: 865 us; the launch traced here: 864 us
  waiting for transfers between devices  667 us (77%)
  blocking collectives  69.8 us (8%)
  matrix products  62.2 us (7%)
  local copies, waits for them, and re-layouts  23.2 us (3%)
  other arithmetic  17.5 us (2%)
  between operations  14.1 us (2%)
  loops' own time  10.9 us (1%)
    reduce_scatter x1, waiting for transfers between devices, on_device(): lax.psum_scatter(partials, ('dp', 'rep'), scatter_dimension=0, tiled=True)  593 us
    all_gather x1, waiting for transfers between devices, on_device(): full_table = lax.all_gather(half_table, ('dp', 'rep'), axis=0, tiled=True)  73.1 us
    unnamed x1, blocking collectives  69.8 us
    dot_general x16, matrix products, block_sums(): partial_value = jnp.dot(onehot, rows_in, preferred_element_type=jnp.float32)  62.2 us
  transfers between devices with their start and end apart: 2, of which 2 were waited for; matrix products, arithmetic and copies ran while one was open for 0% of the time, Pallas kernels for 0%

commit v1 on v0

v1 whole, which is shorter than its diff:
```python
import jax
import jax.numpy as jnp
from jax import lax
from jax.experimental import pallas as pl
from jax.experimental.pallas import tpu as pltpu
from jax.sharding import PartitionSpec as P

MESH = pl.DeviceIdType.MESH
F32, BF16, I32 = jnp.float32, jnp.bfloat16, jnp.int32

PRIOR = 8.0
ROWS = 2048
E = 512
KB = 128
OWNERS = 64
SLOTS = 48
PITCH = 64
GROUP = 8
GS = GROUP * SLOTS
NG = OWNERS // GROUP
LANES = ROWS // 128

WIDTH = (256, 128, 128)
COL = (0, 256, 384)
CUT = ((0, 48), (48, 48), (96, 32))

NT = (((1,), (1,)), ((), ()))


def iota(shape, dim):
    return lax.broadcasted_iota(I32, shape, dim)


def kernel(rows, codes, hot, cb, newcb, res, pk, r1, crow, s2, acc2, r2, s3, acc3, r3, tb,
           rowbuf, vcol, sc_send, sc_recv, cn1, cr1, cn2, cr2, cn3, cr3, cx, cxr,
           tot3, tot3r, nb, nbr, slot, picks, psend,
           rs_s, rs_r, sc_s, sc_r, cn_s, cn_r, ag_s, ag_r, x_s, x_r, p_s, p_r):
    d = lax.axis_index("dp")
    r = lax.axis_index("rep")
    x, y, z = lax.rem(d, 4), lax.rem(d // 4, 4), d // 16
    mine = (x, y, z)
    stride = (1, 4, 16)
    sibling = (d, 1 - r)

    def pick(seq, u, stage):
        a, b = seq[(u + stage) % 3], seq[(u + stage + 1) % 3]
        return a + r * (b - a)

    def digits(coords, u):
        return tuple(pick(coords, u, stage) for stage in range(3))

    def peer(u, stage, k):
        c = pick(mine, u, stage)
        there = lax.rem(c + k, 4)
        return (d + (there - c) * pick(stride, u, stage), r), there

    my_digits = [digits(mine, u) for u in range(3)]

    barrier = pltpu.get_barrier_semaphore()
    for axis in range(3):
        for k in range(1, 4):
            there = lax.rem(mine[axis] + k, 4)
            pl.semaphore_signal(barrier, inc=1, device_id=(d + (there - mine[axis]) * stride[axis], r),
                                device_id_type=MESH)
    pl.semaphore_signal(barrier, inc=1, device_id=sibling, device_id_type=MESH)

    hot_id = jnp.broadcast_to(hot[:, 0:1], (256, 128))
    hot_to = jnp.broadcast_to(hot[:, 1:2] + 1, (256, 128)).astype(F32)
    odd = lax.rem(iota((1, 128), 1), 2) == 1
    before = jnp.where(iota((128, 128), 0) < iota((128, 128), 1), 1.0, 0.0).astype(BF16)
    owner_id = iota((OWNERS, 128), 0)
    carry = jnp.zeros((OWNERS, 128), F32)
    for b in range(LANES):
        lanes = slice(b * 128, (b + 1) * 128)
        code = codes[b:b + 1, :]
        partner = jnp.sum(jnp.where(hot_id == code, hot_to, 0.0), axis=0, keepdims=True)
        code = jnp.where(odd & (partner > 0.0), partner.astype(I32) - 1, code)
        owner = code // KB
        mark = jnp.where(owner_id == owner, 1.0, 0.0)
        ahead = jnp.dot(mark.astype(BF16), before, preferred_element_type=F32) + carry
        rank = jnp.sum(mark * ahead, axis=0, keepdims=True)
        carry = carry + jnp.sum(mark, axis=1, keepdims=True)
        owner_f = owner.astype(F32)
        rowbuf[0:1, lanes] = owner_f * SLOTS + rank
        rowbuf[1:2, lanes] = owner_f
        rowbuf[2:3, lanes] = rank
        rowbuf[3:4, lanes] = (code - owner * KB).astype(F32)

    for u in range(3):
        r1[u][:, :, SLOTS:, :] = jnp.zeros((16, 4, PITCH - SLOTS, WIDTH[u]), BF16)

    one, zero = jnp.ones((), BF16), jnp.zeros((), BF16)
    slot_iota = (iota((GS, 128), 0) - GS // 2).astype(F32).astype(BF16)

    def slot_rows(group):
        middle = (group * GS + GS // 2).astype(F32)
        tiles = []
        for b in range(LANES):
            v = jnp.broadcast_to(rowbuf[0:1, b * 128:(b + 1) * 128] - middle, (16, 128)).astype(BF16)
            v = jnp.concatenate([v] * (GS // 16), axis=0)
            tiles.append(jnp.where(v == slot_iota, one, zero))
        return jnp.concatenate(tiles, axis=1)

    pl.semaphore_wait(barrier, 10)

    def pack(step, _):
        oz = lax.rem(z + 1 + step // 2, 4)
        half = lax.rem(step, 2)
        packed = jnp.dot(slot_rows(oz * 2 + half), rows[...], preferred_element_type=F32).astype(BF16)
        for j in range(GROUP):
            where = (j % 4, half * 2 + j // 4, oz)
            for u in range(3):
                c1, c2, c3 = digits(where, u)
                at, sub = c1 * 16 + c2 * 4 + c3, c2 * 4 + c3
                k = lax.rem(c1 - my_digits[u][0] + 4, 4)
                pk[u][at] = packed[j * SLOTS:(j + 1) * SLOTS, COL[u]:COL[u] + WIDTH[u]]
                src, dst = pk[u].at[at], r1[u].at[sub, k, pl.ds(0, SLOTS)]

                @pl.when(k == 0)
                def _():
                    pltpu.make_async_copy(src, dst, rs_r.at[u, 0, 0]).start()

                @pl.when(k != 0)
                def _():
                    to = (d + (c1 - my_digits[u][0]) * pick(stride, u, 0), r)
                    pltpu.make_async_remote_copy(src, dst, rs_s.at[u, 0, k], rs_r.at[u, 0, k], device_id=to,
                                                 device_id_type=MESH).start()
        return 0

    lax.fori_loop(0, NG, pack, 0)

    o = rowbuf[1:2, :].astype(I32)
    coords = (lax.rem(o, 4), lax.rem(o // 4, 4), o // 16)

    def lane_tiles(f):
        return jnp.concatenate([f(slice(b * 128, (b + 1) * 128)) for b in range(LANES)], axis=1)

    id128 = iota((128, 128), 0).astype(F32)
    rank_mark = lane_tiles(lambda s: jnp.where(rowbuf[2:3, s] == id128, 1.0, 0.0).astype(BF16))
    low_mark = lane_tiles(lambda s: jnp.where(rowbuf[3:4, s] == id128, 1.0, 0.0).astype(BF16))

    def small_copy(src, dst, ss, rs, to):
        return pltpu.make_async_remote_copy(src, dst, ss, rs, device_id=to, device_id_type=MESH)

    sc_copies, cn_copies = {}, {}
    for u in range(3):
        c1, c2, c3 = digits(coords, u)
        place = c1 * 16 + c2 * 4 + c3
        low = lane_tiles(lambda s: jnp.where(place[:, s] == owner_id, rowbuf[3:4, s] + 1.0, 0.0).astype(BF16))
        sc = lax.dot_general(low, rank_mark, NT, preferred_element_type=F32).astype(BF16)
        for c in range(4):
            sc_send[u, c] = sc[c * 16:(c + 1) * 16]
        for k in range(1, 4):
            to, there = peer(u, 0, k)
            sc_copies[u, k] = small_copy(sc_send.at[u, there], sc_recv.at[u, k], sc_s.at[u, k], sc_r.at[u, k], to)
            sc_copies[u, k].start()
        if u == 0:
            own = lane_tiles(lambda s: jnp.where(place[:, s] == owner_id, 1.0, 0.0).astype(BF16))
            cn = lax.dot_general(own, low_mark, NT, preferred_element_type=F32)
            for c in range(4):
                cn1[c] = cn[c * 16:(c + 1) * 16]
            for k in range(1, 4):
                to, there = peer(0, 0, k)
                cn_copies[0, k] = small_copy(cn1.at[there], cr1.at[k], cn_s.at[0, k], cn_r.at[0, k], to)
                cn_copies[0, k].start()

    low_wide = lane_tiles(
        lambda s: jnp.concatenate([jnp.broadcast_to(rowbuf[3:4, s] + 1.0, (16, 128)).astype(BF16)] * 8, axis=0))

    def slot_code(g, _):
        slot[0, pl.ds(g * GS, GS)] = lax.dot_general(
            slot_rows(g), low_wide, NT, preferred_element_type=F32).astype(BF16)
        return 0

    lax.fori_loop(0, NG, slot_code, 0)
    slot_copy = small_copy(slot.at[0], slot.at[1], x_s.at[3], x_r.at[3], sibling)
    slot_copy.start()
    for b in range(LANES):
        v = jnp.broadcast_to(rowbuf[0:1, b * 128:(b + 1) * 128], (128, 128))
        vcol[b * 128:(b + 1) * 128, :] = jnp.transpose(v)

    code_id = (iota((KB, 256), 0) + 1).astype(F32)
    s1_copies, s2_copies, s3_copies = {}, {}, {}
    for u in range(3):
        for k in range(1, 4):
            to, there = peer(u, 0, k)
            s1_copies[u, k] = pltpu.make_async_remote_copy(
                pk[u].at[pl.ds(there * 16, 16)], r1[u].at[:, k, pl.ds(0, SLOTS)], rs_s.at[u, 0, k],
                rs_r.at[u, 0, k], device_id=to, device_id_type=MESH)
    for u in (1, 2, 0):
        c1, c2, c3 = my_digits[u]
        pltpu.make_async_copy(pk[u].at[pl.ds(c1 * 16, 16)], r1[u].at[:, 0, pl.ds(0, SLOTS)],
                              rs_r.at[u, 0, 0]).wait()
        for k in range(1, 4):
            s1_copies[u, k].wait_recv()
            sc_copies[u, k].wait_recv()
        quarter = [sc_send[u, c1].astype(F32)] + [sc_recv[u, k].astype(F32) for k in range(1, 4)]
        crow[u, :, 0:128] = quarter[0] + pltpu.roll(quarter[1], 64, 1)
        crow[u, :, 128:256] = quarter[2] + pltpu.roll(quarter[3], 64, 1)
        for q in (1, 3, 2, 0):
            to, there = peer(u, 1, q)
            for t in range(4):
                j = there * 4 + t
                mark = jnp.where(code_id == crow[u, pl.ds(j, 1), :], 1.0, 0.0).astype(BF16)
                part = jnp.dot(mark, r1[u][j].reshape(4 * PITCH, WIDTH[u]), preferred_element_type=F32)
                if q == 0:
                    acc2[u][t] = part
                else:
                    s2[u][q - 1, t] = part.astype(BF16)
            if q:
                s2_copies[u, q] = small_copy(s2[u].at[q - 1], r2[u].at[q - 1], rs_s.at[u, 1, q], rs_r.at[u, 1, q], to)
                s2_copies[u, q].start()
        if u == 0:
            total = cn1[c1]
            for k in range(1, 4):
                cn_copies[0, k].wait_recv()
                total = total + cr1[k]
            cn2[...] = total
            for k in range(1, 4):
                cn_copies[1, k] = small_copy(cn2, cr2.at[k - 1], cn_s.at[1, k], cn_r.at[1, k], peer(0, 1, k)[0])
                cn_copies[1, k].start()

    for u in (1, 2, 0):
        for q in range(1, 4):
            s2_copies[u, q].wait_recv()
        for q in (1, 3, 2, 0):
            to, there = peer(u, 2, q)
            part = acc2[u][there]
            for k in range(3):
                part = part + r2[u][k, there].astype(F32)
            if q == 0:
                acc3[u][...] = part
            else:
                s3[u][q - 1] = part.astype(BF16)
                s3_copies[u, q] = small_copy(s3[u].at[q - 1], r3[u].at[q - 1], rs_s.at[u, 2, q], rs_r.at[u, 2, q], to)
                s3_copies[u, q].start()
        if u == 0:
            total = cn2[...]
            for k in range(1, 4):
                cn_copies[1, k].wait_recv()
                total = total + cr2[k - 1]
            cn3[...] = total
            for k in range(1, 4):
                cn_copies[2, k] = small_copy(cn3, cr3.at[k - 1], cn_s.at[2, k], cn_r.at[2, k], peer(0, 2, k)[0])
                cn_copies[2, k].start()

    for u in (1, 2, 0):
        part = acc3[u][...]
        for q in range(1, 4):
            s3_copies[u, q].wait_recv()
            part = part + r3[u][q - 1].astype(F32)
        if u == 0:
            tot3[0] = part
        else:
            tot3[1, :, (u - 1) * 128:u * 128] = part
    total = cn3[...]
    for k in range(1, 4):
        cn_copies[2, k].wait_recv()
        total = total + cr3[k - 1]
    mine_at = my_digits[0][1] * 4 + my_digits[0][2]
    cx[...] = jnp.broadcast_to(
        jnp.sum(jnp.where(iota((16, 128), 0) == mine_at, total, 0.0), axis=0, keepdims=True), (8, 128))
    tot_copy = small_copy(tot3.at[1 - r], tot3r, x_s.at[0], x_r.at[0], sibling)
    cx_copy = small_copy(cx, cxr, x_s.at[1], x_r.at[1], sibling)
    cx_copy.start()
    tot_copy.start()
    cx_copy.wait_recv()
    count = cx[0:1, :] + cxr[0:1, :]
    diagonal = iota((128, 128), 0) == iota((128, 128), 1)
    count = jnp.sum(jnp.where(diagonal, jnp.broadcast_to(count, (128, 128)), 0.0), axis=1, keepdims=True)
    old = jnp.where(r == 0, cb[:, :256], cb[:, 256:])
    tot_copy.wait_recv()
    new = (tot3[r] + tot3r[...] + PRIOR * old) / (count + PRIOR)
    low_new = new.astype(BF16)
    ag = {}
    for u in range(3):
        c1, c2, c3 = my_digits[u]
        tb[u][c1 * 16 + c2 * 4 + c3] = low_new[CUT[u][0]:CUT[u][0] + CUT[u][1]]

    for stage, size in ((2, 1), (1, 4), (0, 16)):
        for u in range(3):
            c1, c2, c3 = my_digits[u]
            first = c1 * 16 + (c2 * 4 if size < 16 else 0) + (c3 if size < 4 else 0)
            block = tb[u].at[pl.ds(first, size)]
            if stage < 2:
                for k in range(1, 4):
                    ag[u, stage + 1, k].wait_recv()
            for k in range(1, 4):
                ag[u, stage, k] = small_copy(block, block, ag_s.at[u, stage, k], ag_r.at[u, stage, k],
                                             peer(u, stage, k)[0])
                ag[u, stage, k].start()
        if stage == 2:
            nb[0] = new[:64]
            nb[1] = new[64:]
            new_copy = small_copy(nb.at[1 - r], nbr, x_s.at[2], x_r.at[2], sibling)
            new_copy.start()
    new_copy.wait_recv()
    kept = nb[r]
    newcb[:, :256] = jnp.where(r == 0, kept, nbr[...])
    newcb[:, 256:] = jnp.where(r == 0, nbr[...], kept)
    slot_copy.wait_recv()
    for u in range(3):
        for k in range(1, 4):
            ag[u, 0, k].wait_recv()

    lane_code = (iota((SLOTS, 128), 1) + 1).astype(F32).astype(BF16)

    def take(g, _):
        for j in range(GROUP):
            where = (j % 4, lax.rem(g, 2) * 2 + j // 4, g // 2)
            parts = []
            for u in range(3):
                c1, c2, c3 = digits(where, u)
                parts.append(tb[u][c1 * 16 + c2 * 4 + c3])
            at = pl.ds(g * GS + j * SLOTS, SLOTS)
            mark = jnp.concatenate(
                [jnp.where(slot[0, at] == lane_code, one, zero), jnp.where(slot[1, at] == lane_code, one, zero)], axis=0)
            got = jnp.dot(mark, jnp.concatenate(parts, axis=0), preferred_element_type=F32).astype(BF16)
            picks[r, at] = got[:SLOTS]
            psend[at] = got[SLOTS:]
        at = pl.ds(g * GS, GS)
        small_copy(psend.at[at], picks.at[r, at], p_s.at[0], p_r.at[0], sibling).start()
        return 0

    lax.fori_loop(0, NG, take, 0)
    p_copy = small_copy(psend, picks.at[1 - r], p_s.at[0], p_r.at[0], sibling)
    p_copy.wait_recv()

    lane_slot = [(iota((256, 128), 1) + (128 * t - GS // 2)).astype(F32).astype(BF16) for t in range(GS // 128)]

    def unpack(m, _):
        at = pl.ds(m * 256, 256)
        v = vcol[at, :]
        tiles = []
        for g in range(NG):
            w = (v - (g * GS + GS // 2)).astype(BF16)
            for t in range(GS // 128):
                tiles.append(jnp.where(w == lane_slot[t], one, zero))
        mark = jnp.concatenate(tiles, axis=1)
        for h in range(2):
            cols = slice(h * 256, (h + 1) * 256)
            got = jnp.dot(mark, picks[h], preferred_element_type=F32)
            res[at, cols] = (rows[at, cols].astype(F32) - got).astype(BF16)
        return 0

    lax.fori_loop(0, ROWS // 256, unpack, 0)

    for group in (s1_copies, sc_copies, cn_copies, s2_copies, s3_copies, ag):
        for copy in group.values():
            copy.wait_send()
    for copy in (tot_copy, cx_copy, new_copy, slot_copy, p_copy):
        copy.wait_send()


def on_device(rows_in, row_codes, hot_split, codebook):
    vm = pltpu.VMEM
    dma = pltpu.SemaphoreType.DMA
    whole = pl.BlockSpec(memory_space=pltpu.VMEM)
    scratch = [
        tuple(vm((OWNERS, SLOTS, w), BF16) for w in WIDTH),
        tuple(vm((16, 4, PITCH, w), BF16) for w in WIDTH),
        vm((3, 16, 256), F32),
        tuple(vm((3, 4, KB, w), BF16) for w in WIDTH),
        tuple(vm((4, KB, w), F32) for w in WIDTH),
        tuple(vm((3, 4, KB, w), BF16) for w in WIDTH),
        tuple(vm((3, KB, w), BF16) for w in WIDTH),
        tuple(vm((KB, w), F32) for w in WIDTH),
        tuple(vm((3, KB, w), BF16) for w in WIDTH),
        tuple(vm((OWNERS, n, 256), BF16) for _, n in CUT),
        vm((8, ROWS), F32),
        vm((ROWS, 128), F32),
        vm((3, 4, 16, 128), BF16),
        vm((3, 4, 16, 128), BF16),
        vm((4, 16, 128), F32),
        vm((4, 16, 128), F32),
        vm((16, 128), F32),
        vm((3, 16, 128), F32),
        vm((16, 128), F32),
        vm((3, 16, 128), F32),
        vm((8, 128), F32),
        vm((8, 128), F32),
        vm((2, KB, 256), F32),
        vm((KB, 256), F32),
        vm((2, 64, 256), F32),
        vm((64, 256), F32),
        vm((2, OWNERS * SLOTS, 128), BF16),
        vm((2, OWNERS * SLOTS, 256), BF16),
        vm((OWNERS * SLOTS, 256), BF16),
        dma((3, 3, 4)), dma((3, 3, 4)),
        dma((3, 4)), dma((3, 4)),
        dma((3, 4)), dma((3, 4)),
        dma((3, 3, 4)), dma((3, 3, 4)),
        dma((4,)), dma((4,)),
        dma((1,)), dma((1,)),
    ]
    return pl.pallas_call(
        kernel,
        out_shape=(jax.ShapeDtypeStruct((KB // 2, E), F32), jax.ShapeDtypeStruct((ROWS, E), BF16)),
        in_specs=[whole] * 4,
        out_specs=(whole, whole),
        scratch_shapes=scratch,
        compiler_params=pltpu.CompilerParams(collective_id=0, has_side_effects=True,
                                             vmem_limit_bytes=56 * 2**20),
    )(rows_in, row_codes.reshape(LANES, 128), hot_split, codebook)


def solution(mesh):
    return jax.shard_map(
        on_device,
        mesh=mesh,
        in_specs=(P(("dp", "rep"), None), P(("dp", "rep")), P(), P("dp", None)),
        out_specs=(P(("dp", "rep"), None), P(("dp", "rep"), None)),
        check_vma=False,
    )
```

time: 865 us -> 96.8 us (0.11)
  waiting for transfers between devices: 667 us -> 0 us
  Pallas kernels: 0 us -> 89.9 us
  blocking collectives: 69.8 us -> 0 us
  matrix products: 62.2 us -> 0 us
  other arithmetic: 17.5 us -> 0 us
  local copies, waits for them, and re-layouts: 23.2 us -> 6.09 us
  between operations: 14.1 us -> 0.64 us
  loops' own time: 10.9 us -> 0 us
    reduce_scatter x1 -> x0, waiting for transfers between devices: 593 us -> none  [on_device(): lax.psum_scatter(partials, ('dp', 'rep'), scatter_dimension=0, tiled=True)]
    pallas_call x0 -> x1, Pallas kernels: none -> 89.9 us  [on_device(): pl.pallas_call(kernel, out_shape=(jax.ShapeDtypeStruct((KB // 2, E), F32)...]
    all_gather x1 -> x0, waiting for transfers between devices: 73.1 us -> none  [on_device(): full_table = lax.all_gather(half_table, ('dp', 'rep'), axis=0, tiled=True)]
    unnamed x1 -> x0, blocking collectives: 69.8 us -> none
    dot_general x16 -> x0, matrix products: 62.2 us -> none  [block_sums(): partial_value = jnp.dot(onehot, rows_in, preferred_element_type=jnp.float32)]
    gather x1 -> x0, local copies, waits for them, and re-layouts: 12 us -> none  [on_device(): picked = full_table[codes].astype(jnp.float32)]
    another operation x1 -> x0, loops' own time: 10.9 us -> none  [on_device(): lax.map(block_sums, jnp.arange(all_codes // block_size, dtype=jnp.int32))]
    reduce_sum x17 -> x0, other arithmetic: 10.2 us -> none  [the longest x16 8.75 us: block_sums(): tally = jnp.sum(onehot, axis=1, dtype=jnp.float32)]
  transfers between devices with their start and end apart: 2 -> 0, of which waited for: 2 -> 0; matrix products, arithmetic and copies ran while one was open for 0% -> 0% of each run, Pallas kernels for 0% -> 0%
where the time goes in v1:
time: 96.8 us; the launch traced here: 96.6 us
  Pallas kernels  89.9 us (93%)
  local copies, waits for them, and re-layouts  6.09 us (6%)
    pallas_call x1, Pallas kernels, on_device(): pl.pallas_call(kernel, out_shape=(jax.ShapeDtypeStruct((KB // 2, E), F32)...  89.9 us
    unnamed x3, local copies, waits for them, and re-layouts  6.09 us

profile of v1, /device:TPU:1, one launch (start us, length us, event | category | flops | bytes accessed | tf_op | source)
XLA Modules:
  0.0 96.6 jit_solution(5325547545697880550)
XLA Ops:
  0.6 1.5 %copy.6.hot = s32[256,2]{1,0:T(8,128)} copy(s32[256,2]{0,1:T(2,128)} %param.6) | data formatting | bytes 4096 | tf_op args[2]
  2.1 89.9 %shard_map.59 = (f32[64,512]{1,0:T(8,128)}, bf16[2048,512]{1,0:T(8,128)(2,1)}) custom-call(bf16[2048,512]{1,0:T(8,128)(2,1)} %rows.1, s32[16,128]{1,0:T(8,128)} %bitcast.1, s32[256,2]{1,0:T(8,128)} %copy.6.hot, f32[128,512]{1,0:T(8,128)} %cb.1), custom_call_target="tpu_custom_call" | custom-call | tf_op jit(solution)/shard_map/pallas_call | solution.py:396
  92.0 1.6 %copy.9 = f32[64,512]{1,0:T(8,128)} copy(f32[64,512]{1,0:T(8,128)} %get-tuple-element.4) | data formatting | bytes 262144
  93.6 3.0 %copy.10 = bf16[2048,512]{1,0:T(8,128)(2,1)} copy(bf16[2048,512]{1,0:T(8,128)(2,1)} %get-tuple-element.5) | data formatting | bytes 4194304

commit v2 on v1

v2 whole, which is shorter than its diff:
```python
import jax
import jax.numpy as jnp
from jax import lax
from jax.experimental import pallas as pl
from jax.experimental.pallas import tpu as pltpu
from jax.sharding import PartitionSpec as P

MESH = pl.DeviceIdType.MESH
F32, BF16, I32 = jnp.float32, jnp.bfloat16, jnp.int32

PRIOR = 8.0
ROWS = 2048
E = 512
KB = 128
OWNERS = 64
SLOTS = 48
PITCH = 64
GROUP = 8
GS = GROUP * SLOTS
NG = OWNERS // GROUP
LANES = ROWS // 128

WIDTH = (256, 128, 128)
COL = (0, 256, 384)
CUT = ((0, 48), (48, 48), (96, 32))

NEAR = 27
NEAR_KEPT = 24

NT = (((1,), (1,)), ((), ()))


def iota(shape, dim):
    return lax.broadcasted_iota(I32, shape, dim)


def kernel(rows_hbm, codes, hot, cb, newcb, res, rows, pk, r1, crow, s2, acc2, r2, s3, acc3, r3, tb,
           rowbuf, vcol, sc_send, sc_recv, cn1, cr1, cn2, cr2, cn3, cr3, cx, cxr,
           tot3, tot3r, nb, nbr, slot, picks, psend, held, out,
           in_s, out_s, rs_s, rs_r, sc_s, sc_r, cn_s, cn_r, ag_s, ag_r, x_s, x_r, p_s, p_r):
    d = lax.axis_index("dp")
    r = lax.axis_index("rep")
    x, y, z = lax.rem(d, 4), lax.rem(d // 4, 4), d // 16
    mine = (x, y, z)
    stride = (1, 4, 16)
    sibling = (d, 1 - r)

    def pick(seq, u, stage):
        a, b = seq[(u + stage) % 3], seq[(u + stage + 1) % 3]
        return a + r * (b - a)

    def digits(coords, u):
        return tuple(pick(coords, u, stage) for stage in range(3))

    def peer(u, stage, k):
        c = pick(mine, u, stage)
        there = lax.rem(c + k, 4)
        return (d + (there - c) * pick(stride, u, stage), r), there

    my_digits = [digits(mine, u) for u in range(3)]

    rows_copy = pltpu.make_async_copy(rows_hbm, rows, in_s)
    rows_copy.start()

    barrier = pltpu.get_barrier_semaphore()
    for axis in range(3):
        for k in range(1, 4):
            there = lax.rem(mine[axis] + k, 4)
            pl.semaphore_signal(barrier, inc=1, device_id=(d + (there - mine[axis]) * stride[axis], r),
                                device_id_type=MESH)
    pl.semaphore_signal(barrier, inc=1, device_id=sibling, device_id_type=MESH)

    def down(row):
        return jnp.transpose(jnp.broadcast_to(row, (128, 128)))

    hot_f = hot[...].astype(F32)
    hot_id = jnp.concatenate([down(hot_f[0:1, :128]), down(hot_f[0:1, 128:])], axis=0).astype(I32)
    hot_to = jnp.concatenate([down(hot_f[1:2, :128]), down(hot_f[1:2, 128:])], axis=0) + 1.0
    def order(owner):
        dx = lax.rem(owner + (4 - x), 4)
        dy = lax.rem(owner // 4 + (4 - y), 4)
        dz = lax.rem(owner // 16 + (4 - z), 4)
        ey, ez = dy - dy // 3, dz - dz // 3
        near = ez * 9 + ey * 3 + dx - dx // 3
        far = jnp.where(dz == 2, dy * 4 + dx, jnp.where(dy == 2, 16 + ez * 4 + dx, 28 + ez * 3 + ey))
        return jnp.where((dx == 2) | (dy == 2) | (dz == 2), NEAR + far, near)

    odd = lax.rem(iota((1, 128), 1), 2) == 1
    before = jnp.where(iota((128, 128), 0) < iota((128, 128), 1), 1.0, 0.0).astype(BF16)
    owner_id = iota((OWNERS, 128), 0)
    carry = jnp.zeros((OWNERS, 128), F32)
    for b in range(LANES):
        lanes = slice(b * 128, (b + 1) * 128)
        code = codes[b:b + 1, :]
        partner = jnp.sum(jnp.where(hot_id == code, hot_to, 0.0), axis=0, keepdims=True)
        code = jnp.where(odd & (partner > 0.0), partner.astype(I32) - 1, code)
        owner = code // KB
        mark = jnp.where(owner_id == owner, 1.0, 0.0)
        ahead = jnp.dot(mark.astype(BF16), before, preferred_element_type=F32) + carry
        rank = jnp.sum(mark * ahead, axis=0, keepdims=True)
        carry = carry + jnp.sum(mark, axis=1, keepdims=True)
        owner_f = owner.astype(F32)
        rowbuf[0:1, lanes] = owner_f * SLOTS + rank
        rowbuf[1:2, lanes] = owner_f
        rowbuf[2:3, lanes] = rank
        rowbuf[3:4, lanes] = (code - owner * KB).astype(F32)
        rowbuf[4:5, lanes] = order(owner).astype(F32) * SLOTS + rank

    for u in range(3):
        r1[u][:, :, :, SLOTS:, :] = jnp.zeros((4, 4, 4, PITCH - SLOTS, WIDTH[u]), BF16)

    one, zero = jnp.ones((), BF16), jnp.zeros((), BF16)
    slot_iota = (iota((GS, 128), 0) - GS // 2).astype(F32).astype(BF16)

    def slot_rows(group, kind):
        middle = (group * GS + GS // 2).astype(F32)
        tiles = []
        for b in range(LANES):
            v = jnp.broadcast_to(rowbuf[kind:kind + 1, b * 128:(b + 1) * 128] - middle, (16, 128)).astype(BF16)
            v = jnp.concatenate([v] * (GS // 16), axis=0)
            tiles.append(jnp.where(v == slot_iota, one, zero))
        return jnp.concatenate(tiles, axis=1)

    rows_copy.wait()
    pl.semaphore_wait(barrier, 10)
    def remote(src, dst, ss, rs, to):
        return pltpu.make_async_remote_copy(src, dst, ss, rs, device_id=to, device_id_type=MESH)

    s1_copies = {}
    for u in range(3):
        for k in range(1, 4):
            to, there = peer(u, 0, k)
            s1_copies[u, k] = remote(
                pk[u].at[there], r1[u].at[:, :, k, pl.ds(0, SLOTS)], rs_s.at[u, 0, k],
                rs_r.at[u, 0, k], to)

    def send_plane(oz, away, core):
        for u in range(3):
            first = (u + core) % 3
            if first == 2:
                dz = lax.rem(oz - z + 4, 4)
                src, dst = pk[u].at[oz], r1[u].at[:, :, dz, pl.ds(0, SLOTS)]

                @pl.when(away)
                def _():
                    remote(src, dst, rs_s.at[u, 0, dz], rs_r.at[u, 0, dz], (d + (oz - z) * 16, r)).start()

                @pl.when(jnp.logical_not(away))
                def _():
                    pltpu.make_async_copy(src, dst, rs_r.at[u, 0, 0]).start()
            else:
                for k in (2, 1, 3, 0):
                    to, there = peer(u, 0, k)
                    if first == 0:
                        src, dst = pk[u].at[there, :, oz], r1[u].at[:, oz, k, pl.ds(0, SLOTS)]
                    else:
                        src, dst = pk[u].at[there, oz], r1[u].at[oz, :, k, pl.ds(0, SLOTS)]
                    if k:
                        remote(src, dst, rs_s.at[u, 0, k], rs_r.at[u, 0, k], to).start()
                    else:
                        pltpu.make_async_copy(src, dst, rs_r.at[u, 0, 0]).start()

    def pack(step, _):
        oz = lax.rem(z + 2 + 3 * step, 4)
        for half in range(2):
            packed = jnp.dot(slot_rows(oz * 2 + half, 0), rows[...], preferred_element_type=F32).astype(BF16)
            for j in range(GROUP):
                where = (j % 4, half * 2 + j // 4, oz)
                for u in range(3):
                    c1, c2, c3 = digits(where, u)
                    pk[u][c1, c2, c3] = packed[j * SLOTS:(j + 1) * SLOTS, COL[u]:COL[u] + WIDTH[u]]
        for core in range(2):
            @pl.when(r == core)
            def _():
                send_plane(oz, oz != z, core)
        return 0

    lax.fori_loop(0, 4, pack, 0)

    o = rowbuf[1:2, :].astype(I32)
    coords = (lax.rem(o, 4), lax.rem(o // 4, 4), o // 16)

    def lane_tiles(f):
        return jnp.concatenate([f(slice(b * 128, (b + 1) * 128)) for b in range(LANES)], axis=1)

    id128 = iota((128, 128), 0).astype(F32)
    rank_mark = lane_tiles(lambda s: jnp.where(rowbuf[2:3, s] == id128, 1.0, 0.0).astype(BF16))
    low_mark = lane_tiles(lambda s: jnp.where(rowbuf[3:4, s] == id128, 1.0, 0.0).astype(BF16))

    sc_copies, cn_copies = {}, {}
    for u in range(3):
        c1, c2, c3 = digits(coords, u)
        place = c1 * 16 + c2 * 4 + c3
        low = lane_tiles(lambda s: jnp.where(place[:, s] == owner_id, rowbuf[3:4, s] + 1.0, 0.0).astype(BF16))
        sc = lax.dot_general(low, rank_mark, NT, preferred_element_type=F32).astype(BF16)
        for c in range(4):
            sc_send[u, c] = sc[c * 16:(c + 1) * 16]
        for k in range(1, 4):
            to, there = peer(u, 0, k)
            sc_copies[u, k] = remote(sc_send.at[u, there], sc_recv.at[u, k], sc_s.at[u, k], sc_r.at[u, k], to)
            sc_copies[u, k].start()
        if u == 0:
            own = lane_tiles(lambda s: jnp.where(place[:, s] == owner_id, 1.0, 0.0).astype(BF16))
            cn = lax.dot_general(own, low_mark, NT, preferred_element_type=F32)
            for c in range(4):
                cn1[c] = cn[c * 16:(c + 1) * 16]
            for k in range(1, 4):
                to, there = peer(0, 0, k)
                cn_copies[0, k] = remote(cn1.at[there], cr1.at[k], cn_s.at[0, k], cn_r.at[0, k], to)
                cn_copies[0, k].start()

    low_wide = lane_tiles(
        lambda s: jnp.concatenate([jnp.broadcast_to(rowbuf[3:4, s] + 1.0, (16, 128)).astype(BF16)] * 8, axis=0))

    def slot_code(g, _):
        slot[0, pl.ds(g * GS, GS)] = lax.dot_general(
            slot_rows(g, 4), low_wide, NT, preferred_element_type=F32).astype(BF16)
        return 0

    lax.fori_loop(0, NG, slot_code, 0)
    slot_copy = remote(slot.at[0], slot.at[1], x_s.at[3], x_r.at[3], sibling)
    slot_copy.start()
    for b in range(LANES):
        v = jnp.broadcast_to(rowbuf[4:5, b * 128:(b + 1) * 128], (128, 128))
        vcol[b * 128:(b + 1) * 128, :] = jnp.transpose(v)

    code_id = (iota((KB, 256), 0) + 1).astype(F32)
    s2_copies, s3_copies = {}, {}
    for u in (1, 2, 0):
        c1, c2, c3 = my_digits[u]
        pltpu.make_async_copy(pk[u].at[c1], r1[u].at[:, :, 0, pl.ds(0, SLOTS)],
                              rs_r.at[u, 0, 0]).wait()
        for k in range(1, 4):
            s1_copies[u, k].wait_recv()
            sc_copies[u, k].wait_recv()
        quarter = [sc_send[u, c1].astype(F32)] + [sc_recv[u, k].astype(F32) for k in range(1, 4)]
        crow[u, :, 0:128] = quarter[0] + pltpu.roll(quarter[1], 64, 1)
        crow[u, :, 128:256] = quarter[2] + pltpu.roll(quarter[3], 64, 1)
        for q in (1, 3, 2, 0):
            to, there = peer(u, 1, q)
            for t in range(4):
                j = there * 4 + t
                mark = jnp.where(code_id == crow[u, pl.ds(j, 1), :], 1.0, 0.0).astype(BF16)
                part = jnp.dot(mark, r1[u][there, t].reshape(4 * PITCH, WIDTH[u]), preferred_element_type=F32)
                if q == 0:
                    acc2[u][t] = part
                else:
                    s2[u][q - 1, t] = part.astype(BF16)
            if q:
                s2_copies[u, q] = remote(s2[u].at[q - 1], r2[u].at[q - 1], rs_s.at[u, 1, q], rs_r.at[u, 1, q], to)
                s2_copies[u, q].start()
        if u == 0:
            total = cn1[c1]
            for k in range(1, 4):
                cn_copies[0, k].wait_recv()
                total = total + cr1[k]
            cn2[...] = total
            for k in range(1, 4):
                cn_copies[1, k] = remote(cn2, cr2.at[k - 1], cn_s.at[1, k], cn_r.at[1, k], peer(0, 1, k)[0])
                cn_copies[1, k].start()

    for u in (1, 2, 0):
        for q in range(1, 4):
            s2_copies[u, q].wait_recv()
        for q in (1, 3, 2, 0):
            to, there = peer(u, 2, q)
            part = acc2[u][there]
            for k in range(3):
                part = part + r2[u][k, there].astype(F32)
            if q == 0:
                acc3[u][...] = part
            else:
                s3[u][q - 1] = part.astype(BF16)
                s3_copies[u, q] = remote(s3[u].at[q - 1], r3[u].at[q - 1], rs_s.at[u, 2, q], rs_r.at[u, 2, q], to)
                s3_copies[u, q].start()
        if u == 0:
            total = cn2[...]
            for k in range(1, 4):
                cn_copies[1, k].wait_recv()
                total = total + cr2[k - 1]
            cn3[...] = total
            for k in range(1, 4):
                cn_copies[2, k] = remote(cn3, cr3.at[k - 1], cn_s.at[2, k], cn_r.at[2, k], peer(0, 2, k)[0])
                cn_copies[2, k].start()

    for u in (1, 2, 0):
        part = acc3[u][...]
        for q in range(1, 4):
            s3_copies[u, q].wait_recv()
            part = part + r3[u][q - 1].astype(F32)
        if u == 0:
            tot3[0] = part
        else:
            tot3[1, :, (u - 1) * 128:u * 128] = part
    total = cn3[...]
    for k in range(1, 4):
        cn_copies[2, k].wait_recv()
        total = total + cr3[k - 1]
    mine_at = my_digits[0][1] * 4 + my_digits[0][2]
    cx[...] = jnp.broadcast_to(
        jnp.sum(jnp.where(iota((16, 128), 0) == mine_at, total, 0.0), axis=0, keepdims=True), (8, 128))
    tot_copy = remote(tot3.at[1 - r], tot3r, x_s.at[0], x_r.at[0], sibling)
    cx_copy = remote(cx, cxr, x_s.at[1], x_r.at[1], sibling)
    cx_copy.start()
    tot_copy.start()
    cx_copy.wait_recv()
    count = cx[0:1, :] + cxr[0:1, :]
    diagonal = iota((128, 128), 0) == iota((128, 128), 1)
    count = jnp.sum(jnp.where(diagonal, jnp.broadcast_to(count, (128, 128)), 0.0), axis=1, keepdims=True)
    old = jnp.where(r == 0, cb[:, :256], cb[:, 256:])
    tot_copy.wait_recv()
    new = (tot3[r] + tot3r[...] + PRIOR * old) / (count + PRIOR)
    low_new = new.astype(BF16)
    for u in range(3):
        c1, c2, c3 = my_digits[u]
        tb[u][c1, c2, c3] = low_new[CUT[u][0]:CUT[u][0] + CUT[u][1]]
    nb[0] = new[:64]
    nb[1] = new[64:]

    ag = {}

    def gather(u, stage, tag, k, block, lane):
        copy = remote(block, block, ag_s.at[u, lane], ag_r.at[u, lane], peer(u, stage, k)[0])
        copy.start()
        ag[(u,) + tag] = copy

    def line(u, e1, e2, half=None):
        c1, c2, c3 = my_digits[u]
        i1, i2 = lax.rem(c1 + e1, 4), lax.rem(c2 + e2, 4)
        return tb[u].at[i1, i2] if half is None else tb[u].at[i1, i2, pl.ds(2 * half, 2)]

    def both_ways(u, stage, tag, block, lane):
        gather(u, stage, tag + (1,), 1, block, lane)
        gather(u, stage, tag + (3,), 3, block, lane + 1)

    def pass_on(u, stage, tag, e1, e2, lane):
        step = {0: ((e1 + 3) % 4, (e1 + 1) % 4, e2, e2), 1: (e1, e1, (e2 + 3) % 4, (e2 + 1) % 4)}[stage]
        ag[(u,) + tag + (1,)].wait_recv()
        gather(u, stage, tag + ("up",), 1, line(u, step[0], step[2], 0), lane + 2)
        ag[(u,) + tag + (3,)].wait_recv()
        gather(u, stage, tag + ("down",), 3, line(u, step[1], step[3], 1), lane + 3)

    for u in range(3):
        c1, c2, c3 = my_digits[u]
        for k in range(1, 4):
            gather(u, 2, ("a", k), k, tb[u].at[c1, c2, c3], k - 1)
    new_copy = remote(nb.at[1 - r], nbr, x_s.at[2], x_r.at[2], sibling)
    new_copy.start()
    for u in range(3):
        for k in range(1, 4):
            ag[u, "a", k].wait_recv()
        both_ways(u, 1, ("b",), line(u, 0, 0), 4)
        both_ways(u, 0, ("c", 0), line(u, 0, 0), 8)
    new_copy.wait_recv()
    kept = nb[r]
    newcb[:, :256] = jnp.where(r == 0, kept, nbr[...])
    newcb[:, 256:] = jnp.where(r == 0, nbr[...], kept)
    for u in range(3):
        pass_on(u, 1, ("b",), 0, 0, 4)
        both_ways(u, 0, ("c", 1), line(u, 0, 1), 12)
        both_ways(u, 0, ("c", 3), line(u, 0, 3), 16)
    for u in range(3):
        pass_on(u, 0, ("c", 0), 0, 0, 8)
    for u in range(3):
        ag[u, "b", "up"].wait_recv()
        ag[u, "b", "down"].wait_recv()
        both_ways(u, 0, ("c", 2), line(u, 0, 2), 20)
    for u in range(3):
        pass_on(u, 0, ("c", 1), 0, 1, 12)
        pass_on(u, 0, ("c", 3), 0, 3, 16)
    slot_copy.wait_recv()

    lane_code = (iota((SLOTS, 128), 1) + 1).astype(F32).astype(BF16)

    def take(first, steps, sem):
        for j, step in enumerate(steps):
            where = tuple(lax.rem(c + e, 4) for c, e in zip(mine, step))
            parts = []
            for u in range(3):
                c1, c2, c3 = digits(where, u)
                parts.append(tb[u][c1, c2, c3])
            at = pl.ds((first + j) * SLOTS, SLOTS)
            mark = jnp.concatenate(
                [jnp.where(slot[0, at] == lane_code, one, zero), jnp.where(slot[1, at] == lane_code, one, zero)], axis=0)
            got = jnp.dot(mark, jnp.concatenate(parts, axis=0), preferred_element_type=F32).astype(BF16)
            picks[r, at] = got[:SLOTS]
            psend[at] = got[SLOTS:]
        at = pl.ds(first * SLOTS, len(steps) * SLOTS)
        remote(psend.at[at], picks.at[r, at], p_s.at[sem], p_r.at[sem], sibling).start()

    def near(ez, _):
        take(ez * 9, [((0, 1, 3)[i % 3], (0, 1, 3)[i // 3], ez + ez // 2) for i in range(9)], 0)
        return 0

    lax.fori_loop(0, 3, near, 0)
    for u in range(3):
        pass_on(u, 0, ("c", 2), 0, 2, 20)

    def slot_marks(at, begin, end):
        v = vcol[at, :]
        tiles = []
        for g in range(begin // GROUP, end // GROUP):
            w = (v - (g * GS + GS // 2)).astype(BF16)
            for t in range(GS // 128):
                tiles.append(jnp.where(w == lane_slot[t], one, zero))
        return jnp.concatenate(tiles, axis=1)

    lane_slot = [(iota((256, 128), 1) + (128 * t - GS // 2)).astype(F32).astype(BF16) for t in range(GS // 128)]
    near_rows = pl.ds(0, NEAR * SLOTS)
    far_rows = pl.ds(NEAR * SLOTS, (OWNERS - NEAR) * SLOTS)
    p_copies = [remote(psend.at[at], picks.at[1 - r, at], p_s.at[i], p_r.at[i], sibling)
                for i, at in enumerate((near_rows, far_rows))]
    p_copies[0].wait_recv()

    def unpack_near(m, _):
        at = pl.ds(m * 256, 256)
        mark = slot_marks(at, 0, NEAR_KEPT)
        for h in range(2):
            got = jnp.dot(mark, picks[h, 0:NEAR_KEPT * SLOTS], preferred_element_type=F32)
            held[h, at] = got.astype(BF16)
        return 0

    lax.fori_loop(0, ROWS // 256, unpack_near, 0)
    for u in range(3):
        for e in range(4):
            ag[u, "c", e, "up"].wait_recv()
            ag[u, "c", e, "down"].wait_recv()

    def far_z(dy, _):
        take(NEAR + dy * 4, [(i, dy, 2) for i in range(4)], 1)
        return 0

    def far_y(ez, _):
        take(NEAR + 16 + ez * 4, [(i, 2, ez + ez // 2) for i in range(4)], 1)
        return 0

    def far_x(ez, _):
        take(NEAR + 28 + ez * 3, [(2, (0, 1, 3)[i], ez + ez // 2) for i in range(3)], 1)
        return 0

    lax.fori_loop(0, 4, far_z, 0)
    lax.fori_loop(0, 3, far_y, 0)
    lax.fori_loop(0, 3, far_x, 0)

    outs = []
    for turn in range(2):
        h = r + turn * (1 - 2 * r)
        cols = pl.ds(pl.multiple_of(h * 256, 256), 256)
        if turn:
            p_copies[1].wait_recv()

        def unpack(m, _):
            at = pl.ds(m * 256, 256)
            mark = slot_marks(at, NEAR_KEPT, OWNERS)
            got = jnp.dot(mark, picks[h, NEAR_KEPT * SLOTS:], preferred_element_type=F32)
            got = got + held[h, at].astype(F32)
            out[h, at] = (rows[at, cols].astype(F32) - got).astype(BF16)
            pltpu.make_async_copy(out.at[h, at], res.at[at, cols], out_s.at[turn]).start()
            return 0

        lax.fori_loop(0, ROWS // 256, unpack, 0)
        outs.append(pltpu.make_async_copy(out.at[h], res.at[:, cols], out_s.at[turn]))
    for copy in outs:
        copy.wait()

    for group in (s1_copies, sc_copies, cn_copies, s2_copies, s3_copies, ag):
        for copy in group.values():
            copy.wait_send()
    for copy in [tot_copy, cx_copy, new_copy, slot_copy] + p_copies:
        copy.wait_send()


def hand_over(new, residual):
    parts = 4

    def copy(new_in, res_in, new_out, res_out, new_buf, res_buf, sems):
        def moves(i):
            if i == parts:
                return (pltpu.make_async_copy(new_in, new_buf, sems.at[0, i]),
                        pltpu.make_async_copy(new_buf, new_out, sems.at[1, i]))
            at = pl.ds(i * (ROWS // parts), ROWS // parts)
            return (pltpu.make_async_copy(res_in.at[at], res_buf.at[at], sems.at[0, i]),
                    pltpu.make_async_copy(res_buf.at[at], res_out.at[at], sems.at[1, i]))

        pairs = [moves(i) for i in range(parts + 1)]
        for there, _ in pairs:
            there.start()
        for there, back in pairs:
            there.wait()
            back.start()
        for _, back in pairs:
            back.wait()

    anywhere = pl.BlockSpec(memory_space=pl.ANY)
    return pl.pallas_call(
        copy,
        out_shape=(jax.ShapeDtypeStruct(new.shape, new.dtype), jax.ShapeDtypeStruct(residual.shape, residual.dtype)),
        in_specs=[anywhere] * 2,
        out_specs=(anywhere, anywhere),
        scratch_shapes=[pltpu.VMEM(new.shape, new.dtype), pltpu.VMEM(residual.shape, residual.dtype),
                        pltpu.SemaphoreType.DMA((2, parts + 1))],
    )(new, residual)


def on_device(rows_in, row_codes, hot_split, codebook):
    vm = pltpu.VMEM
    dma = pltpu.SemaphoreType.DMA
    whole = pl.BlockSpec(memory_space=pltpu.VMEM)
    scratch = [
        vm((ROWS, E), BF16),
        tuple(vm((4, 4, 4, SLOTS, w), BF16) for w in WIDTH),
        tuple(vm((4, 4, 4, PITCH, w), BF16) for w in WIDTH),
        vm((3, 16, 256), F32),
        tuple(vm((3, 4, KB, w), BF16) for w in WIDTH),
        tuple(vm((4, KB, w), F32) for w in WIDTH),
        tuple(vm((3, 4, KB, w), BF16) for w in WIDTH),
        tuple(vm((3, KB, w), BF16) for w in WIDTH),
        tuple(vm((KB, w), F32) for w in WIDTH),
        tuple(vm((3, KB, w), BF16) for w in WIDTH),
        tuple(vm((4, 4, 4, n, 256), BF16) for _, n in CUT),
        vm((8, ROWS), F32),
        vm((ROWS, 128), F32),
        vm((3, 4, 16, 128), BF16),
        vm((3, 4, 16, 128), BF16),
        vm((4, 16, 128), F32),
        vm((4, 16, 128), F32),
        vm((16, 128), F32),
        vm((3, 16, 128), F32),
        vm((16, 128), F32),
        vm((3, 16, 128), F32),
        vm((8, 128), F32),
        vm((8, 128), F32),
        vm((2, KB, 256), F32),
        vm((KB, 256), F32),
        vm((2, 64, 256), F32),
        vm((64, 256), F32),
        vm((2, OWNERS * SLOTS, 128), BF16),
        vm((2, OWNERS * SLOTS, 256), BF16),
        vm((OWNERS * SLOTS, 256), BF16),
        vm((2, ROWS, 256), BF16),
        vm((2, ROWS, 256), BF16),
        dma, dma((2,)),
        dma((3, 3, 4)), dma((3, 3, 4)),
        dma((3, 4)), dma((3, 4)),
        dma((3, 4)), dma((3, 4)),
        dma((3, 24)), dma((3, 24)),
        dma((4,)), dma((4,)),
        dma((2,)), dma((2,)),
    ]
    new, residual = pl.pallas_call(
        kernel,
        out_shape=(jax.ShapeDtypeStruct((KB // 2, E), F32), jax.ShapeDtypeStruct((ROWS, E), BF16)),
        in_specs=[pl.BlockSpec(memory_space=pl.ANY)] + [whole] * 3,
        out_specs=(whole, pl.BlockSpec(memory_space=pl.ANY)),
        scratch_shapes=scratch,
        compiler_params=pltpu.CompilerParams(collective_id=0, has_side_effects=True,
                                             vmem_limit_bytes=56 * 2**20),
    )(rows_in, row_codes.reshape(LANES, 128), hot_split.T, codebook)
    return hand_over(new, residual)


def solution(mesh):
    return jax.shard_map(
        on_device,
        mesh=mesh,
        in_specs=(P(("dp", "rep"), None), P(("dp", "rep")), P(), P("dp", None)),
        out_specs=(P(("dp", "rep"), None), P(("dp", "rep"), None)),
        check_vma=False,
    )
```

time: 96.8 us -> 80.9 us (0.84)
  Pallas kernels: 89.9 us -> 80.1 us
  local copies, waits for them, and re-layouts: 6.09 us -> 0 us
    pallas_call x1, Pallas kernels: 89.9 us -> 77.6 us  [on_device(): pl.pallas_call(kernel, out_shape=(jax.ShapeDtypeStruct((KB // 2, E), F32)...]
    unnamed x3 -> x0, local copies, waits for them, and re-layouts: 6.09 us -> none
    pallas_call x0 -> x1, Pallas kernels: none -> 2.47 us  [hand_over(): pl.pallas_call(copy, out_shape=(jax.ShapeDtypeStruct(new.shape, new.dtype...]
where the time goes in v2:
time: 80.9 us; the launch traced here: 80.7 us
  Pallas kernels  80.1 us (99%)
    pallas_call x1, Pallas kernels, on_device(): pl.pallas_call(kernel, out_shape=(jax.ShapeDtypeStruct((KB // 2, E), F32)...  77.6 us
    pallas_call x1, Pallas kernels, hand_over(): pl.pallas_call(copy, out_shape=(jax.ShapeDtypeStruct(new.shape, new.dtype...  2.47 us

profile of v2, /device:TPU:1, one launch (start us, length us, event | category | flops | bytes accessed | tf_op | source)
XLA Modules:
  0.0 80.7 jit_solution(12666581989938843001)
XLA Ops:
  0.6 77.6 %shard_map.59 = (f32[64,512]{1,0:T(8,128)}, bf16[2048,512]{1,0:T(8,128)(2,1)}) custom-call(bf16[2048,512]{1,0:T(8,128)(2,1)} %rows_hbm.1, s32[16,128]{1,0:T(8,128)} %bitcast.2, s32[2,256]{1,0:T(2,128)} %bitcast.3, f32[128,512]{1,0:T(8,128)} %cb.1), custom_call_target="tpu_custom_call" | custom-call | tf_op jit(solution)/shard_map/pallas_call | solution.py:550
  78.3 2.5 %shard_map.60 = (f32[64,512]{1,0:T(8,128)}, bf16[2048,512]{1,0:T(8,128)(2,1)}) custom-call(f32[64,512]{1,0:T(8,128)} %get-tuple-element.4.new_in, bf16[2048,512]{1,0:T(8,128)(2,1)} %get-tuple-element.5.res_in), custom_call_target="tpu_custom_call" | custom-call | tf_op jit(solution)/shard_map/pallas_call | solution.py:495

commit v3 on v2

--- a/solution.py
+++ b/solution.py
@@ -34,10 +34,10 @@
     return lax.broadcasted_iota(I32, shape, dim)
 
 
-def kernel(rows_hbm, codes, hot, cb, newcb, res, rows, pk, r1, crow, s2, acc2, r2, s3, acc3, r3, tb,
+def kernel(rows_hbm, codes_hbm, hot_hbm, cb_hbm, newcb, res, rows, codes, hot, old, new_out, pk, r1, crow, s2, t2, own2, r2, s3, acc3, r3, tb,
            rowbuf, vcol, sc_send, sc_recv, cn1, cr1, cn2, cr2, cn3, cr3, cx, cxr,
            tot3, tot3r, nb, nbr, slot, picks, psend, held, out,
-           in_s, out_s, rs_s, rs_r, sc_s, sc_r, cn_s, cn_r, ag_s, ag_r, x_s, x_r, p_s, p_r):
+           in_s, out_s, w_s, w_r, rs_s, rs_r, sc_s, sc_r, cn_s, cn_r, ag_s, ag_r, x_s, x_r, p_s, p_r):
     d = lax.axis_index("dp")
     r = lax.axis_index("rep")
     x, y, z = lax.rem(d, 4), lax.rem(d // 4, 4), d // 16
@@ -58,9 +58,6 @@
         return (d + (there - c) * pick(stride, u, stage), r), there
 
     my_digits = [digits(mine, u) for u in range(3)]
-
-    rows_copy = pltpu.make_async_copy(rows_hbm, rows, in_s)
-    rows_copy.start()
 
     barrier = pltpu.get_barrier_semaphore()
     for axis in range(3):
@@ -69,6 +66,15 @@
             pl.semaphore_signal(barrier, inc=1, device_id=(d + (there - mine[axis]) * stride[axis], r),
                                 device_id_type=MESH)
     pl.semaphore_signal(barrier, inc=1, device_id=sibling, device_id_type=MESH)
+
+    codes_copy = pltpu.make_async_copy(codes_hbm, codes, in_s.at[0])
+    hot_copy = pltpu.make_async_copy(hot_hbm, hot, in_s.at[1])
+    rows_copy = pltpu.make_async_copy(rows_hbm, rows, in_s.at[2])
+    old_copy = pltpu.make_async_copy(cb_hbm.at[:, pl.ds(pl.multiple_of(r * 256, 256), 256)], old, in_s.at[3])
+    for copy in (codes_copy, hot_copy, rows_copy, old_copy):
+        copy.start()
+    hot_copy.wait()
+    codes_copy.wait()
 
     def down(row):
         return jnp.transpose(jnp.broadcast_to(row, (128, 128)))
@@ -226,6 +232,16 @@
 
     code_id = (iota((KB, 256), 0) + 1).astype(F32)
     s2_copies, s3_copies = {}, {}
+    def ring_sum(u, q, t):
+        there = peer(u, 1, q)[1]
+        mark = jnp.where(code_id == crow[u, pl.ds(there * 4 + t, 1), :], 1.0, 0.0).astype(BF16)
+        return jnp.dot(mark, r1[u][there, t].reshape(4 * PITCH, WIDTH[u]), preferred_element_type=F32)
+
+    def send_sum(u, name, src, dst, lane, k):
+        s2_copies[(u,) + name] = remote(src, dst, w_s.at[u, lane], w_r.at[u, lane], peer(u, 1, k)[0])
+        s2_copies[(u,) + name].start()
+
+    halves = (pl.ds(0, 2), pl.ds(2, 2))
     for u in (1, 2, 0):
         c1, c2, c3 = my_digits[u]
         pltpu.make_async_copy(pk[u].at[c1], r1[u].at[:, :, 0, pl.ds(0, SLOTS)],
@@ -236,36 +252,47 @@
         quarter = [sc_send[u, c1].astype(F32)] + [sc_recv[u, k].astype(F32) for k in range(1, 4)]
         crow[u, :, 0:128] = quarter[0] + pltpu.roll(quarter[1], 64, 1)
         crow[u, :, 128:256] = quarter[2] + pltpu.roll(quarter[3], 64, 1)
-        for q in (1, 3, 2, 0):
-            to, there = peer(u, 1, q)
-            for t in range(4):
-                j = there * 4 + t
-                mark = jnp.where(code_id == crow[u, pl.ds(j, 1), :], 1.0, 0.0).astype(BF16)
-                part = jnp.dot(mark, r1[u][there, t].reshape(4 * PITCH, WIDTH[u]), preferred_element_type=F32)
-                if q == 0:
-                    acc2[u][t] = part
-                else:
-                    s2[u][q - 1, t] = part.astype(BF16)
-            if q:
-                s2_copies[u, q] = remote(s2[u].at[q - 1], r2[u].at[q - 1], rs_s.at[u, 1, q], rs_r.at[u, 1, q], to)
-                s2_copies[u, q].start()
-        if u == 0:
-            total = cn1[c1]
-            for k in range(1, 4):
-                cn_copies[0, k].wait_recv()
-                total = total + cr1[k]
-            cn2[...] = total
-            for k in range(1, 4):
-                cn_copies[1, k] = remote(cn2, cr2.at[k - 1], cn_s.at[1, k], cn_r.at[1, k], peer(0, 1, k)[0])
-                cn_copies[1, k].start()
-
+        parts = [ring_sum(u, 2, t).astype(BF16) for t in range(4)]
+        for t in range(4):
+            s2[u][1, t] = parts[t]
+        for half in range(2):
+            send_sum(u, ("via", half), s2[u].at[1, halves[half]], t2[u].at[half], half, (1, 3)[half])
     for u in (1, 2, 0):
-        for q in range(1, 4):
-            s2_copies[u, q].wait_recv()
+        order2 = ((1, 2), (1, 3), (3, 0), (3, 1))
+        parts = [ring_sum(u, q, t).astype(BF16) for q, t in order2]
+        for (q, t), part in zip(order2, parts):
+            s2[u][q - 1, t] = part
+        for half, q in ((1, 1), (0, 3)):
+            send_sum(u, ("whole", q), s2[u].at[q - 1, halves[half]], r2[u].at[q // 2, halves[half]], 2 + q // 2, q)
+    u, c1 = 0, my_digits[0][0]
+    total = cn1[c1]
+    for k in range(1, 4):
+        cn_copies[0, k].wait_recv()
+        total = total + cr1[k]
+    cn2[...] = total
+    for k in range(1, 4):
+        cn_copies[1, k] = remote(cn2, cr2.at[k - 1], cn_s.at[1, k], cn_r.at[1, k], peer(0, 1, k)[0])
+        cn_copies[1, k].start()
+
+    for u in (1, 2, 0):
+        for half, q in ((0, 1), (1, 3)):
+            parts = [ring_sum(u, q, 2 * half + t) for t in range(2)]
+            s2_copies[u, "via", half].wait_recv()
+            for t in range(2):
+                s2[u][q - 1, 2 * half + t] = (parts[t] + t2[u][half, t].astype(F32)).astype(BF16)
+            send_sum(u, ("added", q), s2[u].at[q - 1, halves[half]], r2[u].at[q // 2, halves[half]], 4 + q // 2, q)
+    for u in (1, 2, 0):
+        for t in range(4):
+            own2[u][t] = ring_sum(u, 0, t)
+
+    for u in (1, 2, 0):
+        for name in ("whole", "added"):
+            for q in (1, 3):
+                s2_copies[u, name, q].wait_recv()
         for q in (1, 3, 2, 0):
             to, there = peer(u, 2, q)
-            part = acc2[u][there]
-            for k in range(3):
+            part = own2[u][there]
+            for k in range(2):
                 part = part + r2[u][k, there].astype(F32)
             if q == 0:
                 acc3[u][...] = part
@@ -307,9 +334,9 @@
     count = cx[0:1, :] + cxr[0:1, :]
     diagonal = iota((128, 128), 0) == iota((128, 128), 1)
     count = jnp.sum(jnp.where(diagonal, jnp.broadcast_to(count, (128, 128)), 0.0), axis=1, keepdims=True)
-    old = jnp.where(r == 0, cb[:, :256], cb[:, 256:])
+    old_copy.wait()
     tot_copy.wait_recv()
-    new = (tot3[r] + tot3r[...] + PRIOR * old) / (count + PRIOR)
+    new = (tot3[r] + tot3r[...] + PRIOR * old[...]) / (count + PRIOR)
     low_new = new.astype(BF16)
     for u in range(3):
         c1, c2, c3 = my_digits[u]
@@ -353,8 +380,10 @@
         both_ways(u, 0, ("c", 0), line(u, 0, 0), 8)
     new_copy.wait_recv()
     kept = nb[r]
-    newcb[:, :256] = jnp.where(r == 0, kept, nbr[...])
-    newcb[:, 256:] = jnp.where(r == 0, nbr[...], kept)
+    new_out[:, :256] = jnp.where(r == 0, kept, nbr[...])
+    new_out[:, 256:] = jnp.where(r == 0, nbr[...], kept)
+    new_out_copy = pltpu.make_async_copy(new_out, newcb, out_s.at[2])
+    new_out_copy.start()
     for u in range(3):
         pass_on(u, 1, ("b",), 0, 0, 4)
         both_ways(u, 0, ("c", 1), line(u, 0, 1), 12)
@@ -373,18 +402,21 @@
     lane_code = (iota((SLOTS, 128), 1) + 1).astype(F32).astype(BF16)
 
     def take(first, steps, sem):
-        for j, step in enumerate(steps):
-            where = tuple(lax.rem(c + e, 4) for c, e in zip(mine, step))
-            parts = []
-            for u in range(3):
-                c1, c2, c3 = digits(where, u)
-                parts.append(tb[u][c1, c2, c3])
-            at = pl.ds((first + j) * SLOTS, SLOTS)
-            mark = jnp.concatenate(
-                [jnp.where(slot[0, at] == lane_code, one, zero), jnp.where(slot[1, at] == lane_code, one, zero)], axis=0)
-            got = jnp.dot(mark, jnp.concatenate(parts, axis=0), preferred_element_type=F32).astype(BF16)
-            picks[r, at] = got[:SLOTS]
-            psend[at] = got[SLOTS:]
+        for begin in range(0, len(steps), 3):
+            found = []
+            for j in range(begin, min(begin + 3, len(steps))):
+                where = tuple(lax.rem(c + e, 4) for c, e in zip(mine, steps[j]))
+                parts = []
+                for u in range(3):
+                    c1, c2, c3 = digits(where, u)
+                    parts.append(tb[u][c1, c2, c3])
+                at = pl.ds((first + j) * SLOTS, SLOTS)
+                mark = jnp.concatenate([jnp.where(slot[i, at] == lane_code, one, zero) for i in range(2)], axis=0)
+                got = jnp.dot(mark, jnp.concatenate(parts, axis=0), preferred_element_type=F32)
+                found.append((at, got.astype(BF16)))
+            for at, got in found:
+                picks[r, at] = got[:SLOTS]
+                psend[at] = got[SLOTS:]
         at = pl.ds(first * SLOTS, len(steps) * SLOTS)
         remote(psend.at[at], picks.at[r, at], p_s.at[sem], p_r.at[sem], sibling).start()
 
@@ -460,6 +492,7 @@
 
         lax.fori_loop(0, ROWS // 256, unpack, 0)
         outs.append(pltpu.make_async_copy(out.at[h], res.at[:, cols], out_s.at[turn]))
+    new_out_copy.wait()
     for copy in outs:
         copy.wait()
 
@@ -505,15 +538,20 @@
 def on_device(rows_in, row_codes, hot_split, codebook):
     vm = pltpu.VMEM
     dma = pltpu.SemaphoreType.DMA
-    whole = pl.BlockSpec(memory_space=pltpu.VMEM)
+    anywhere = pl.BlockSpec(memory_space=pl.ANY)
     scratch = [
         vm((ROWS, E), BF16),
+        vm((LANES, 128), I32),
+        vm((2, 256), I32),
+        vm((KB, 256), F32),
+        vm((KB // 2, E), F32),
         tuple(vm((4, 4, 4, SLOTS, w), BF16) for w in WIDTH),
         tuple(vm((4, 4, 4, PITCH, w), BF16) for w in WIDTH),
         vm((3, 16, 256), F32),
         tuple(vm((3, 4, KB, w), BF16) for w in WIDTH),
+        tuple(vm((2, 2, KB, w), BF16) for w in WIDTH),
         tuple(vm((4, KB, w), F32) for w in WIDTH),
-        tuple(vm((3, 4, KB, w), BF16) for w in WIDTH),
+        tuple(vm((2, 4, KB, w), BF16) for w in WIDTH),
         tuple(vm((3, KB, w), BF16) for w in WIDTH),
         tuple(vm((KB, w), F32) for w in WIDTH),
         tuple(vm((3, KB, w), BF16) for w in WIDTH),
@@ -539,7 +577,8 @@
         vm((OWNERS * SLOTS, 256), BF16),
         vm((2, ROWS, 256), BF16),
         vm((2, ROWS, 256), BF16),
-        dma, dma((2,)),
+        dma((4,)), dma((3,)),
+        dma((3, 6)), dma((3, 6)),
         dma((3, 3, 4)), dma((3, 3, 4)),
         dma((3, 4)), dma((3, 4)),
         dma((3, 4)), dma((3, 4)),
@@ -550,8 +589,8 @@
     new, residual = pl.pallas_call(
         kernel,
         out_shape=(jax.ShapeDtypeStruct((KB // 2, E), F32), jax.ShapeDtypeStruct((ROWS, E), BF16)),
-        in_specs=[pl.BlockSpec(memory_space=pl.ANY)] + [whole] * 3,
-        out_specs=(whole, pl.BlockSpec(memory_space=pl.ANY)),
+        in_specs=[anywhere] * 4,
+        out_specs=(anywhere, anywhere),
         scratch_shapes=scratch,
         compiler_params=pltpu.CompilerParams(collective_id=0, has_side_effects=True,
                                              vmem_limit_bytes=56 * 2**20),

time: 80.9 us -> 79.8 us (0.986)
  Pallas kernels: 80.1 us -> 78.9 us
    pallas_call x1, Pallas kernels: 77.6 us -> 76.4 us  [on_device(): pl.pallas_call(kernel, out_shape=(jax.ShapeDtypeStruct((KB // 2, E), F32)...]
where the time goes in v3:
time: 79.8 us; the launch traced here: 79.6 us
  Pallas kernels  78.9 us (99%)
    pallas_call x1, Pallas kernels, on_device(): pl.pallas_call(kernel, out_shape=(jax.ShapeDtypeStruct((KB // 2, E), F32)...  76.4 us
    pallas_call x1, Pallas kernels, hand_over(): pl.pallas_call(copy, out_shape=(jax.ShapeDtypeStruct(new.shape, new.dtype...  2.47 us

profile of v3, /device:TPU:1, one launch (start us, length us, event | category | flops | bytes accessed | tf_op | source)
XLA Modules:
  0.0 79.6 jit_solution(9226578427696814519)
XLA Ops:
  0.6 76.4 %shard_map.59 = (f32[64,512]{1,0:T(8,128)}, bf16[2048,512]{1,0:T(8,128)(2,1)}) custom-call(bf16[2048,512]{1,0:T(8,128)(2,1)} %rows_hbm.1, s32[16,128]{1,0:T(8,128)} %bitcast.2, s32[2,256]{1,0:T(2,128)} %bitcast.3, f32[128,512]{1,0:T(8,128)} %cb_hbm.1), custom_call_target="tpu_custom_call" | custom-call | tf_op jit(solution)/shard_map/pallas_call | solution.py:589
  77.1 2.5 %shard_map.60 = (f32[64,512]{1,0:T(8,128)}, bf16[2048,512]{1,0:T(8,128)(2,1)}) custom-call(f32[64,512]{1,0:T(8,128)} %get-tuple-element.4.new_in, bf16[2048,512]{1,0:T(8,128)(2,1)} %get-tuple-element.5.res_in), custom_call_target="tpu_custom_call" | custom-call | tf_op jit(solution)/shard_map/pallas_call | solution.py:528

commit v4 on v3

--- a/solution.py
+++ b/solution.py
@@ -12,6 +12,7 @@
 ROWS = 2048
 E = 512
 KB = 128
+BLOCK = 1024
 OWNERS = 64
 SLOTS = 48
 PITCH = 64
@@ -35,7 +36,7 @@
 
 
 def kernel(rows_hbm, codes_hbm, hot_hbm, cb_hbm, newcb, res, rows, codes, hot, old, new_out, pk, r1, crow, s2, t2, own2, r2, s3, acc3, r3, tb,
-           rowbuf, vcol, sc_send, sc_recv, cn1, cr1, cn2, cr2, cn3, cr3, cx, cxr,
+           split, rowbuf, vcol, sc_send, sc_recv, cn1, cr1, cn2, cr2, cn3, cr3, cx, cxr,
            tot3, tot3r, nb, nbr, slot, picks, psend, held, out,
            in_s, out_s, w_s, w_r, rs_s, rs_r, sc_s, sc_r, cn_s, cn_r, ag_s, ag_r, x_s, x_r, p_s, p_r):
     d = lax.axis_index("dp")
@@ -91,27 +92,31 @@
         far = jnp.where(dz == 2, dy * 4 + dx, jnp.where(dy == 2, 16 + ez * 4 + dx, 28 + ez * 3 + ey))
         return jnp.where((dx == 2) | (dy == 2) | (dz == 2), NEAR + far, near)
 
-    odd = lax.rem(iota((1, 128), 1), 2) == 1
+    odd = lax.rem(iota((LANES, 128), 1), 2) == 1
     before = jnp.where(iota((128, 128), 0) < iota((128, 128), 1), 1.0, 0.0).astype(BF16)
     owner_id = iota((OWNERS, 128), 0)
     carry = jnp.zeros((OWNERS, 128), F32)
     for b in range(LANES):
+        hit = jnp.where(hot_id == codes[b:b + 1, :], hot_to, 0.0)
+        split[0, b:b + 1, :] = jnp.sum(hit, axis=0, keepdims=True)
+    partner = split[0]
+    code = jnp.where(odd & (partner > 0.0), partner.astype(I32) - 1, codes[...])
+    owner = code // KB
+    split[1] = owner.astype(F32)
+    split[2] = (code - owner * KB).astype(F32)
+    split[3] = order(owner).astype(F32)
+    for b in range(LANES):
         lanes = slice(b * 128, (b + 1) * 128)
-        code = codes[b:b + 1, :]
-        partner = jnp.sum(jnp.where(hot_id == code, hot_to, 0.0), axis=0, keepdims=True)
-        code = jnp.where(odd & (partner > 0.0), partner.astype(I32) - 1, code)
-        owner = code // KB
-        mark = jnp.where(owner_id == owner, 1.0, 0.0)
+        owner = split[1, b:b + 1, :]
+        mark = jnp.where(owner_id.astype(F32) == owner, 1.0, 0.0)
         ahead = jnp.dot(mark.astype(BF16), before, preferred_element_type=F32) + carry
         rank = jnp.sum(mark * ahead, axis=0, keepdims=True)
         carry = carry + jnp.sum(mark, axis=1, keepdims=True)
-        owner_f = owner.astype(F32)
-        rowbuf[0:1, lanes] = owner_f * SLOTS + rank
-        rowbuf[1:2, lanes] = owner_f
+        rowbuf[0:1, lanes] = owner * SLOTS + rank
+        rowbuf[1:2, lanes] = owner
         rowbuf[2:3, lanes] = rank
-        rowbuf[3:4, lanes] = (code - owner * KB).astype(F32)
-        rowbuf[4:5, lanes] = order(owner).astype(F32) * SLOTS + rank
-
+        rowbuf[3:4, lanes] = split[2, b:b + 1, :]
+        rowbuf[4:5, lanes] = split[3, b:b + 1, :] * SLOTS + rank
     for u in range(3):
         r1[u][:, :, :, SLOTS:, :] = jnp.zeros((4, 4, 4, PITCH - SLOTS, WIDTH[u]), BF16)
 
@@ -140,12 +145,14 @@
                 pk[u].at[there], r1[u].at[:, :, k, pl.ds(0, SLOTS)], rs_s.at[u, 0, k],
                 rs_r.at[u, 0, k], to)
 
-    def send_plane(oz, away, core):
+    def send_half(oz, half, away, core):
+        part = pl.ds(2 * half, 2)
+        slots = pl.ds(0, SLOTS)
         for u in range(3):
             first = (u + core) % 3
             if first == 2:
                 dz = lax.rem(oz - z + 4, 4)
-                src, dst = pk[u].at[oz], r1[u].at[:, :, dz, pl.ds(0, SLOTS)]
+                src, dst = pk[u].at[oz, :, part], r1[u].at[:, part, dz, slots]
 
                 @pl.when(away)
                 def _():
@@ -154,17 +161,22 @@
                 @pl.when(jnp.logical_not(away))
                 def _():
                     pltpu.make_async_copy(src, dst, rs_r.at[u, 0, 0]).start()
-            else:
-                for k in (2, 1, 3, 0):
-                    to, there = peer(u, 0, k)
-                    if first == 0:
-                        src, dst = pk[u].at[there, :, oz], r1[u].at[:, oz, k, pl.ds(0, SLOTS)]
-                    else:
-                        src, dst = pk[u].at[there, oz], r1[u].at[oz, :, k, pl.ds(0, SLOTS)]
+                continue
+            for k in (2, 1, 3, 0):
+                to, there = peer(u, 0, k)
+
+                def send(src, dst):
                     if k:
                         remote(src, dst, rs_s.at[u, 0, k], rs_r.at[u, 0, k], to).start()
                     else:
                         pltpu.make_async_copy(src, dst, rs_r.at[u, 0, 0]).start()
+
+                if first == 0:
+                    send(pk[u].at[there, part, oz], r1[u].at[part, oz, k, slots])
+                else:
+                    @pl.when(there // 2 == half)
+                    def _():
+                        send(pk[u].at[there, oz], r1[u].at[oz, :, k, slots])
 
     def pack(step, _):
         oz = lax.rem(z + 2 + 3 * step, 4)
@@ -175,10 +187,10 @@
                 for u in range(3):
                     c1, c2, c3 = digits(where, u)
                     pk[u][c1, c2, c3] = packed[j * SLOTS:(j + 1) * SLOTS, COL[u]:COL[u] + WIDTH[u]]
-        for core in range(2):
-            @pl.when(r == core)
-            def _():
-                send_plane(oz, oz != z, core)
+            for core in range(2):
+                @pl.when(r == core)
+                def _():
+                    send_half(oz, half, oz != z, core)
         return 0
 
     lax.fori_loop(0, 4, pack, 0)
@@ -437,7 +449,7 @@
                 tiles.append(jnp.where(w == lane_slot[t], one, zero))
         return jnp.concatenate(tiles, axis=1)
 
-    lane_slot = [(iota((256, 128), 1) + (128 * t - GS // 2)).astype(F32).astype(BF16) for t in range(GS // 128)]
+    lane_slot = [(iota((BLOCK, 128), 1) + (128 * t - GS // 2)).astype(F32).astype(BF16) for t in range(GS // 128)]
     near_rows = pl.ds(0, NEAR * SLOTS)
     far_rows = pl.ds(NEAR * SLOTS, (OWNERS - NEAR) * SLOTS)
     p_copies = [remote(psend.at[at], picks.at[1 - r, at], p_s.at[i], p_r.at[i], sibling)
@@ -445,14 +457,14 @@
     p_copies[0].wait_recv()
 
     def unpack_near(m, _):
-        at = pl.ds(m * 256, 256)
+        at = pl.ds(m * BLOCK, BLOCK)
         mark = slot_marks(at, 0, NEAR_KEPT)
         for h in range(2):
             got = jnp.dot(mark, picks[h, 0:NEAR_KEPT * SLOTS], preferred_element_type=F32)
             held[h, at] = got.astype(BF16)
         return 0
 
-    lax.fori_loop(0, ROWS // 256, unpack_near, 0)
+    lax.fori_loop(0, ROWS // BLOCK, unpack_near, 0)
     for u in range(3):
         for e in range(4):
             ag[u, "c", e, "up"].wait_recv()
@@ -482,7 +494,7 @@
             p_copies[1].wait_recv()
 
         def unpack(m, _):
-            at = pl.ds(m * 256, 256)
+            at = pl.ds(m * BLOCK, BLOCK)
             mark = slot_marks(at, NEAR_KEPT, OWNERS)
             got = jnp.dot(mark, picks[h, NEAR_KEPT * SLOTS:], preferred_element_type=F32)
             got = got + held[h, at].astype(F32)
@@ -490,7 +502,7 @@
             pltpu.make_async_copy(out.at[h, at], res.at[at, cols], out_s.at[turn]).start()
             return 0
 
-        lax.fori_loop(0, ROWS // 256, unpack, 0)
+        lax.fori_loop(0, ROWS // BLOCK, unpack, 0)
         outs.append(pltpu.make_async_copy(out.at[h], res.at[:, cols], out_s.at[turn]))
     new_out_copy.wait()
     for copy in outs:
@@ -504,7 +516,7 @@
 
 
 def hand_over(new, residual):
-    parts = 4
+    parts = 8
 
     def copy(new_in, res_in, new_out, res_out, new_buf, res_buf, sems):
         def moves(i):
@@ -556,6 +568,7 @@
         tuple(vm((KB, w), F32) for w in WIDTH),
         tuple(vm((3, KB, w), BF16) for w in WIDTH),
         tuple(vm((4, 4, 4, n, 256), BF16) for _, n in CUT),
+        vm((4, LANES, 128), F32),
         vm((8, ROWS), F32),
         vm((ROWS, 128), F32),
         vm((3, 4, 16, 128), BF16),

time: 79.8 us -> 77.3 us (0.969)
  Pallas kernels: 78.9 us -> 76.2 us
    pallas_call x1, Pallas kernels: 76.4 us -> 73.7 us  [on_device(): pl.pallas_call(kernel, out_shape=(jax.ShapeDtypeStruct((KB // 2, E), F32)...]
where the time goes in v4:
time: 77.3 us; the launch traced here: 76.8 us
  Pallas kernels  76.2 us (99%)
    pallas_call x1, Pallas kernels, on_device(): pl.pallas_call(kernel, out_shape=(jax.ShapeDtypeStruct((KB // 2, E), F32)...  73.7 us
    pallas_call x1, Pallas kernels, hand_over(): pl.pallas_call(copy, out_shape=(jax.ShapeDtypeStruct(new.shape, new.dtype...  2.45 us

profile of v4, /device:TPU:1, one launch (start us, length us, event | category | flops | bytes accessed | tf_op | source)
XLA Modules:
  0.0 76.8 jit_solution(16181027600869908658)
XLA Ops:
  0.6 73.7 %shard_map.59 = (f32[64,512]{1,0:T(8,128)}, bf16[2048,512]{1,0:T(8,128)(2,1)}) custom-call(bf16[2048,512]{1,0:T(8,128)(2,1)} %rows_hbm.1, s32[16,128]{1,0:T(8,128)} %bitcast.2, s32[2,256]{1,0:T(2,128)} %bitcast.3, f32[128,512]{1,0:T(8,128)} %cb_hbm.1), custom_call_target="tpu_custom_call" | custom-call | tf_op jit(solution)/shard_map/pallas_call | solution.py:602
  74.4 2.5 %shard_map.60 = (f32[64,512]{1,0:T(8,128)}, bf16[2048,512]{1,0:T(8,128)(2,1)}) custom-call(f32[64,512]{1,0:T(8,128)} %get-tuple-element.4.new_in, bf16[2048,512]{1,0:T(8,128)(2,1)} %get-tuple-element.5.res_in), custom_call_target="tpu_custom_call" | custom-call | tf_op jit(solution)/shard_map/pallas_call | solution.py:540

commit v5 on v4

--- a/solution.py
+++ b/solution.py
@@ -414,9 +414,9 @@
     lane_code = (iota((SLOTS, 128), 1) + 1).astype(F32).astype(BF16)
 
     def take(first, steps, sem):
-        for begin in range(0, len(steps), 3):
+        for begin in range(0, len(steps), 4):
             found = []
-            for j in range(begin, min(begin + 3, len(steps))):
+            for j in range(begin, min(begin + 4, len(steps))):
                 where = tuple(lax.rem(c + e, 4) for c, e in zip(mine, steps[j]))
                 parts = []
                 for u in range(3):
@@ -482,9 +482,9 @@
         take(NEAR + 28 + ez * 3, [(2, (0, 1, 3)[i], ez + ez // 2) for i in range(3)], 1)
         return 0
 
-    lax.fori_loop(0, 4, far_z, 0)
-    lax.fori_loop(0, 3, far_y, 0)
-    lax.fori_loop(0, 3, far_x, 0)
+    lax.fori_loop(0, 4, far_z, 0, unroll=True)
+    lax.fori_loop(0, 3, far_y, 0, unroll=True)
+    lax.fori_loop(0, 3, far_x, 0, unroll=True)
 
     outs = []
     for turn in range(2):

time: 77.3 us -> 77.3 us (level)
  no operation moved by 1% of the time
where the time goes in v5:
time: 77.3 us; the launch traced here: 76.7 us
  Pallas kernels  76.1 us (98%)
    pallas_call x1, Pallas kernels, on_device(): pl.pallas_call(kernel, out_shape=(jax.ShapeDtypeStruct((KB // 2, E), F32)...  73.7 us
    pallas_call x1, Pallas kernels, hand_over(): pl.pallas_call(copy, out_shape=(jax.ShapeDtypeStruct(new.shape, new.dtype...  2.45 us

profile of v5, /device:TPU:1, one launch (start us, length us, event | category | flops | bytes accessed | tf_op | source)
XLA Modules:
  0.0 76.7 jit_solution(4445899917153402502)
XLA Ops:
  0.6 73.7 %shard_map.59 = (f32[64,512]{1,0:T(8,128)}, bf16[2048,512]{1,0:T(8,128)(2,1)}) custom-call(bf16[2048,512]{1,0:T(8,128)(2,1)} %rows_hbm.1, s32[16,128]{1,0:T(8,128)} %bitcast.2, s32[2,256]{1,0:T(2,128)} %bitcast.3, f32[128,512]{1,0:T(8,128)} %cb_hbm.1), custom_call_target="tpu_custom_call" | custom-call | tf_op jit(solution)/shard_map/pallas_call | solution.py:602
  74.3 2.5 %shard_map.60 = (f32[64,512]{1,0:T(8,128)}, bf16[2048,512]{1,0:T(8,128)(2,1)}) custom-call(f32[64,512]{1,0:T(8,128)} %get-tuple-element.4.new_in, bf16[2048,512]{1,0:T(8,128)(2,1)} %get-tuple-element.5.res_in), custom_call_target="tpu_custom_call" | custom-call | tf_op jit(solution)/shard_map/pallas_call | solution.py:540
